TPU v7x, 32 devices: a whole 2x2x4 slice. The times are simulated.
32 devices in a mesh: dp: 2 (over x), expert: 16 (over z, y, core).
Axes of the slice: x: 2, y: 2, z: 4, core: 2. Of those that a mesh axis runs over, the one named last changes fastest.
Arguments:
- hidden_in: bfloat16 [2, 512, 2048], P(None, ('dp', 'expert')), may hold values from -6 to 6
- cotangent: bfloat16 [2, 512, 2048], P(None, ('dp', 'expert')), may hold values from -6 to 6
- expert_ids: int32 [2, 512, 8], P(None, ('dp', 'expert')), may hold values from 0 to 15, all different within a row; in each aligned block of 16 rows (0 to 15, 16 to 31, ..., all dimensions but the last counted through in order) at most 16 rows name the same one
- route_prob: float32 [2, 512, 8], P(None, ('dp', 'expert')), may hold values from 0.05 to 1
- swap_flags: int32 [8], replicated, may hold values 0 or 1
- gate_up: bfloat16 [16, 2048, 2, 384], P('expert', 'dp'), may hold values from -0.125 to 0.125
- down_t: bfloat16 [16, 2048, 384], P('expert', 'dp'), may hold values from -0.3125 to 0.3125
Outputs:
- hidden_out: bfloat16 [2, 512, 2048], P(None, ('dp', 'expert'))
- input_grad: bfloat16 [2, 512, 2048], P(None, ('dp', 'expert'))
- resident_gate_up: bfloat16 [16, 2048, 2, 384], P('expert', 'dp')
- resident_down: bfloat16 [16, 2048, 384], P('expert', 'dp')
Inputs may be any that keep to these rules, and one draw needn't show every extreme that they name: `expert_ids`: within one microbatch the 16 tokens of one device name any one expert at most 16 times, a bound that some block reaches.
All inputs are finite; a program needn't handle non-finite values.
Results may differ from a plain program's by a relative error of at most 0.0064.
Values may be sent and summed in bfloat16 or wider, within the bound.
A program may use at most 64 MiB of HBM per device.

v0:
```python
import jax
import jax.numpy as jnp
from jax import lax
from jax.sharding import PartitionSpec as P


def from_partner(value, axis, stride):
    mask = 2**stride
    pairs = [(source, source ^ mask) for source in range(lax.axis_size(axis))]
    return lax.ppermute(value, axis, pairs)


def expert_forward(row_block, gate_matrix, down_matrix):
    hidden_width = down_matrix.shape[1]
    projected = jnp.dot(row_block, gate_matrix, preferred_element_type=jnp.float32)
    gate_part = projected[:, :hidden_width]
    upper_part = projected[:, hidden_width:]
    hidden = (jax.nn.silu(gate_part) * upper_part).astype(jnp.bfloat16)
    output = lax.dot_general(
        hidden, down_matrix, (((1,), (1,)), ((), ())), preferred_element_type=jnp.float32
    )
    return (output.astype(jnp.bfloat16), projected)


def expert_backward(grad_block, projected, gate_matrix, down_matrix):
    hidden_width = down_matrix.shape[1]
    gate_part = projected[:, :hidden_width]
    upper_part = projected[:, hidden_width:]
    d_hidden = jnp.dot(grad_block, down_matrix, preferred_element_type=jnp.float32)
    sigmoid_gate = jax.nn.sigmoid(gate_part)
    d_gate = (
        d_hidden * upper_part * sigmoid_gate * (1.0 + gate_part * (1.0 - sigmoid_gate))
    ).astype(jnp.bfloat16)
    d_upper = (d_hidden * gate_part * sigmoid_gate).astype(jnp.bfloat16)
    d_joined = jnp.concatenate([d_gate, d_upper], axis=1)
    d_rows = lax.dot_general(
        d_joined, gate_matrix, (((1,), (1,)), ((), ())), preferred_element_type=jnp.float32
    )
    return d_rows.astype(jnp.bfloat16)


def route_matrix(ids_now, swap_flags, experts, slots, moved):
    token_count, top_count = ids_now.shape
    target = ids_now
    if moved:
        half_axis = experts // 2
        hit_mask = (ids_now % half_axis)[:, :, None] == jnp.arange(half_axis, dtype=jnp.int32)[
            None, None, :
        ]
        flipped = jnp.sum(jnp.where(hit_mask, swap_flags[None, None, :], 0), axis=2)
        target = jnp.where(flipped == 1, ids_now ^ half_axis, ids_now)
    flat_ids = target.reshape(token_count * top_count)
    one_hot = (flat_ids[:, None] == jnp.arange(experts, dtype=jnp.int32)[None, :]).astype(jnp.int32)
    earlier = jnp.cumsum(one_hot, axis=0) - one_hot
    slot_index = jnp.sum(earlier * one_hot, axis=1)
    slot_place = flat_ids * slots + slot_index
    picked = slot_place[:, None] == jnp.arange(experts * slots, dtype=jnp.int32)[None, :]
    return picked.astype(jnp.bfloat16)


def run_micro(tokens_now, grads_now, ids_now, weights_now, swap_flags, gate_full, down_full, moved):
    experts = lax.axis_size("expert")
    token_count, top_count = ids_now.shape
    model_width = tokens_now.shape[1]
    slots = 2 * token_count * top_count // experts
    picked = route_matrix(ids_now, swap_flags, experts, slots, moved)
    by_token = jnp.sum(picked.reshape(token_count, top_count, experts * slots), axis=1)
    first_axis = (((0,), (0,)), ((), ()))
    send_tokens = lax.dot_general(
        by_token, tokens_now, first_axis, preferred_element_type=jnp.float32
    )
    send_tokens = send_tokens.astype(jnp.bfloat16).reshape(experts, slots, model_width)
    row_grads = (weights_now[:, :, None] * grads_now[:, None, :].astype(jnp.float32)).astype(
        jnp.bfloat16
    )
    row_grads = row_grads.reshape(token_count * top_count, model_width)
    send_grads = lax.dot_general(picked, row_grads, first_axis, preferred_element_type=jnp.float32)
    send_grads = send_grads.astype(jnp.bfloat16).reshape(experts, slots, model_width)
    gate_matrix = gate_full.reshape(model_width, -1)
    down_matrix = down_full.reshape(model_width, -1)
    pieces = lax.all_to_all(send_tokens, "expert", split_axis=0, concat_axis=0, tiled=True)
    item_count = pieces.shape[1]
    expert_out, projected = expert_forward(
        pieces.reshape(experts * item_count, model_width), gate_matrix, down_matrix
    )
    returned = lax.all_to_all(
        expert_out.reshape(experts, item_count, model_width),
        "expert",
        split_axis=0,
        concat_axis=0,
        tiled=True,
    )
    saved = projected.reshape(experts, item_count, projected.shape[1])
    arrived = lax.all_to_all(send_grads, "expert", split_axis=0, concat_axis=0, tiled=True)
    row_input = expert_backward(
        arrived.reshape(experts * slots, model_width),
        saved.reshape(experts * slots, saved.shape[2]),
        gate_matrix,
        down_matrix,
    )
    back_grad = lax.all_to_all(
        row_input.reshape(experts, slots, model_width),
        "expert",
        split_axis=0,
        concat_axis=0,
        tiled=True,
    )
    back_rows = jnp.dot(
        picked, returned.reshape(experts * slots, model_width), preferred_element_type=jnp.float32
    )
    back_rows = back_rows.reshape(token_count, top_count, model_width)
    hidden_out = jnp.sum(weights_now[:, :, None] * back_rows, axis=1).astype(jnp.bfloat16)
    back_input = jnp.dot(
        picked, back_grad.reshape(experts * slots, model_width), preferred_element_type=jnp.float32
    )
    input_grad = jnp.sum(back_input.reshape(token_count, top_count, model_width), axis=1).astype(
        jnp.bfloat16
    )
    return (hidden_out, input_grad)


def local(hidden_in, cotangent, expert_ids, route_prob, swap_flags, gate_up, down_t):
    experts = lax.axis_size("expert")
    swap_bit = experts.bit_length() - 2
    half_axis = experts // 2
    my_index = lax.axis_index("expert")
    flag_mine = jnp.sum(
        jnp.where(jnp.arange(half_axis, dtype=jnp.int32) == my_index % half_axis, swap_flags, 0)
    )
    gate_full, down_full = (
        lax.all_gather(gate_up, "dp", axis=1, tiled=True),
        lax.all_gather(down_t, "dp", axis=1, tiled=True),
    )
    out_first, grad_first = run_micro(
        hidden_in[0],
        cotangent[0],
        expert_ids[0],
        route_prob[0],
        swap_flags,
        gate_full,
        down_full,
        False,
    )
    other_gate, other_down = from_partner((gate_up, down_t), "expert", swap_bit)
    resident_gate_up = jnp.where(flag_mine == 1, other_gate, gate_up)
    resident_down = jnp.where(flag_mine == 1, other_down, down_t)
    gate_full, down_full = (
        lax.all_gather(resident_gate_up, "dp", axis=1, tiled=True),
        lax.all_gather(resident_down, "dp", axis=1, tiled=True),
    )
    out_second, grad_second = run_micro(
        hidden_in[1],
        cotangent[1],
        expert_ids[1],
        route_prob[1],
        swap_flags,
        gate_full,
        down_full,
        True,
    )
    return (
        jnp.stack([out_first, out_second]),
        jnp.stack([grad_first, grad_second]),
        resident_gate_up,
        resident_down,
    )


def solution(mesh):
    placed = (
        P(None, ("dp", "expert"), None),
        P(None, ("dp", "expert"), None),
        P(None, ("dp", "expert"), None),
        P(None, ("dp", "expert"), None),
        P(),
        P("expert", "dp", None, None),
        P("expert", "dp", None),
    )
    return jax.shard_map(
        local,
        mesh=mesh,
        in_specs=placed,
        out_specs=(
            P(None, ("dp", "expert"), None),
            P(None, ("dp", "expert"), None),
            P("expert", "dp", None, None),
            P("expert", "dp", None),
        ),
        check_vma=False,
    )
```

profile of v0, /device:TPU:8, one launch (start us, length us, event | category | flops | bytes accessed | tf_op | source)
XLA Modules:
  0.0 365.6 jit_solution(2265351711389331505)
XLA Ops:
  14.3 6.4 %all-to-all-start.2 = ((bf16[16,16,2048]{2,1,0:T(8,128)(2,1)}), bf16[16,16,2048]{2,1,0:T(8,128)(2,1)S(1)}, u32[]{:S(2)}, u32[]{:S(2)}) async-start(bf16[16,16,2048]{2,1,0:T(8,128)(2,1)} %bitcast.16), calls=%async_computation.2 | async-start | bytes 2097152 | tf_op jit(solution)/shard_map/all_to_all | solution.py:81
  23.2 21.7 %all-to-all-done.2 = bf16[16,16,2048]{2,1,0:T(8,128)(2,1)S(1)} async-done(((bf16[16,16,2048]{2,1,0:T(8,128)(2,1)}), bf16[16,16,2048]{2,1,0:T(8,128)(2,1)S(1)}, u32[]{:S(2)}, u32[]{:S(2)}) %all-to-all-start.2) | async-done | bytes 1048608 | tf_op jit(solution)/shard_map/all_to_all | solution.py:81
  45.9 5.6 %all-to-all-start.4 = ((bf16[16,16,2048]{2,1,0:T(8,128)(2,1)}), bf16[16,16,2048]{2,1,0:T(8,128)(2,1)S(1)}, u32[]{:S(2)}, u32[]{:S(2)}) async-start(bf16[16,16,2048]{2,1,0:T(8,128)(2,1)} %bitcast.27), calls=%async_computation.4 | async-start | bytes 2097152 | tf_op jit(solution)/shard_map/all_to_all | solution.py:94
  53.2 22.6 %all-to-all-done.4 = bf16[16,16,2048]{2,1,0:T(8,128)(2,1)S(1)} async-done(((bf16[16,16,2048]{2,1,0:T(8,128)(2,1)}), bf16[16,16,2048]{2,1,0:T(8,128)(2,1)S(1)}, u32[]{:S(2)}, u32[]{:S(2)}) %all-to-all-start.4) | async-done | bytes 1048608 | tf_op jit(solution)/shard_map/all_to_all | solution.py:94
  75.8 5.6 %all-to-all-start = ((bf16[16,16,2048]{2,1,0:T(8,128)(2,1)}), bf16[16,16,2048]{2,1,0:T(8,128)(2,1)}, u32[]{:S(2)}, u32[]{:S(2)}) async-start(bf16[16,16,2048]{2,1,0:T(8,128)(2,1)} %bitcast.4), calls=%async_computation | async-start | bytes 2097152 | tf_op jit(solution)/shard_map/all_to_all | solution.py:81
  86.9 52.5 %all-to-all-done = bf16[16,16,2048]{2,1,0:T(8,128)(2,1)} async-done(((bf16[16,16,2048]{2,1,0:T(8,128)(2,1)}), bf16[16,16,2048]{2,1,0:T(8,128)(2,1)}, u32[]{:S(2)}, u32[]{:S(2)}) %all-to-all-start) | async-done | bytes 1048608 | tf_op jit(solution)/shard_map/all_to_all | solution.py:81
  139.4 6.0 %all-to-all-start.6 = ((bf16[16,16,2048]{2,1,0:T(8,128)(2,1)}), bf16[16,16,2048]{2,1,0:T(8,128)(2,1)}, u32[]{:S(2)}, u32[]{:S(2)}) async-start(bf16[16,16,2048]{2,1,0:T(8,128)(2,1)} %bitcast.35), calls=%async_computation.6 | async-start | bytes 2097152 | tf_op jit(solution)/shard_map/all_to_all | solution.py:94
  145.4 38.4 %collective-permute-done = bf16[1,1024,2,384]{3,2,0,1:T(2,128)(2,1)S(1)} collective-permute-done((bf16[1,1024,2,384]{3,2,0,1:T(2,128)(2,1)S(1)}, bf16[1,1024,2,384]{3,2,0,1:T(2,128)(2,1)S(1)}, u32[]{:S(2)}, u32[]{:S(2)}) %collective-permute-start) | collective-permute-done | bytes 1572896 | tf_op jit(solution)/shard_map/ppermute | solution.py:10
  183.8 2.8 broadcast_select_fusion
  186.6 2.5 copy.74
  189.2 3.1 fusion.56
  192.3 2.7 multiply_convert_fusion.3
  197.0 7.4 %all-to-all-start.5 = ((bf16[16,16,2048]{2,1,0:T(8,128)(2,1)}), bf16[16,16,2048]{2,1,0:T(8,128)(2,1)S(1)}, u32[]{:S(2)}, u32[]{:S(2)}) async-start(bf16[16,16,2048]{2,1,0:T(8,128)(2,1)} %bitcast.132), calls=%async_computation.5 | async-start | bytes 2097152 | tf_op jit(solution)/shard_map/all_to_all | solution.py:101
  207.0 54.4 %collective-permute-done.1 = bf16[1,1024,384]{2,1,0:T(8,128)(2,1)S(1)} collective-permute-done((bf16[1,1024,384]{2,1,0:T(8,128)(2,1)S(1)}, bf16[1,1024,384]{2,1,0:T(8,128)(2,1)S(1)}, u32[]{:S(2)}, u32[]{:S(2)}) %collective-permute-start.1) | collective-permute-done | bytes 786464 | tf_op jit(solution)/shard_map/ppermute | solution.py:10
  262.4 3.2 convolution_convert_fusion.3
  265.6 7.0 %all-to-all-start.1 = ((bf16[16,16,2048]{2,1,0:T(8,128)(2,1)}), bf16[16,16,2048]{2,1,0:T(8,128)(2,1)S(1)}, u32[]{:S(2)}, u32[]{:S(2)}) async-start(bf16[16,16,2048]{2,1,0:T(8,128)(2,1)} %bitcast.8), calls=%async_computation.1 | async-start | bytes 2097152 | tf_op jit(solution)/shard_map/all_to_all | solution.py:86
  272.7 2.8 copy.75
  278.1 13.6 %all-gather.11.cloned.1.call-done = bf16[1,2048,384]{2,1,0:T(8,128)(2,1)} async-done(((bf16[1,1024,384]{2,1,0:T(8,128)(2,1)}), bf16[1,2048,384]{2,1,0:T(8,128)(2,1)}) %all-gather.11.cloned.1.call-update) | async-done | bytes 1572880 | tf_op jit(solution)/shard_map/all_gather | solution.py:149
  291.7 2.6 multiply_convert_fusion.1
  296.8 5.6 %all-to-all-start.7 = ((bf16[16,16,2048]{2,1,0:T(8,128)(2,1)}), bf16[16,16,2048]{2,1,0:T(8,128)(2,1)S(1)}, u32[]{:S(2)}, u32[]{:S(2)}) async-start(bf16[16,16,2048]{2,1,0:T(8,128)(2,1)} %bitcast.134), calls=%async_computation.7 | async-start | bytes 2097152 | tf_op jit(solution)/shard_map/all_to_all | solution.py:101
  302.4 3.4 convolution_convert_fusion.2
  305.8 20.8 %all-to-all-done.7 = bf16[16,16,2048]{2,1,0:T(8,128)(2,1)S(1)} async-done(((bf16[16,16,2048]{2,1,0:T(8,128)(2,1)}), bf16[16,16,2048]{2,1,0:T(8,128)(2,1)S(1)}, u32[]{:S(2)}, u32[]{:S(2)}) %all-to-all-start.7) | async-done | bytes 1048608 | tf_op jit(solution)/shard_map/all_to_all | solution.py:101
  326.7 5.6 %all-to-all-start.3 = ((bf16[16,16,2048]{2,1,0:T(8,128)(2,1)}), bf16[16,16,2048]{2,1,0:T(8,128)(2,1)}, u32[]{:S(2)}, u32[]{:S(2)}) async-start(bf16[16,16,2048]{2,1,0:T(8,128)(2,1)} %bitcast.133), calls=%async_computation.3 | async-start | bytes 2097152 | tf_op jit(solution)/shard_map/all_to_all | solution.py:86
  333.9 22.7 %all-to-all-done.3 = bf16[16,16,2048]{2,1,0:T(8,128)(2,1)} async-done(((bf16[16,16,2048]{2,1,0:T(8,128)(2,1)}), bf16[16,16,2048]{2,1,0:T(8,128)(2,1)}, u32[]{:S(2)}, u32[]{:S(2)}) %all-to-all-start.3) | async-done | bytes 1048608 | tf_op jit(solution)/shard_map/all_to_all | solution.py:86
  (92 shorter events, 31.8 us)
Async XLA Ops:
  14.3 7.2 %copy-start.9 = (f32[2,16,8]{1,2,0:T(8,128)S(1)}, f32[2,16,8]{1,2,0:T(8,128)}, u32[]{:S(2)}) copy-start(f32[2,16,8]{1,2,0:T(8,128)} %param.10) | copy-start | bytes 3076
  14.3 7.2 %copy-start.7 = (bf16[2,16,2048]{2,1,0:T(8,128)(2,1)S(1)}, bf16[2,16,2048]{2,1,0:T(8,128)(2,1)}, u32[]{:S(2)}) copy-start(bf16[2,16,2048]{2,1,0:T(8,128)(2,1)} %param.8) | copy-start | bytes 393220
  14.3 30.7 %all-to-all-start.2 = ((bf16[16,16,2048]{2,1,0:T(8,128)(2,1)}), bf16[16,16,2048]{2,1,0:T(8,128)(2,1)S(1)}, u32[]{:S(2)}, u32[]{:S(2)}) async-start(bf16[16,16,2048]{2,1,0:T(8,128)(2,1)} %bitcast.16), calls=%async_computation.2 | async-start | bytes 2097152 | tf_op jit(solution)/shard_map/all_to_all | solution.py:81
  20.7 165.9 %all-gather.5.cloned.1.call-start = ((), (), s32[]{:S(2)}) async-start(), calls=%async_computation.8 | async-start | bytes 4718592 | tf_op jit(solution)/shard_map/all_gather | solution.py:131
  21.4 30.3 %copy-start.8 = (bf16[2,16,2048]{2,1,0:T(8,128)(2,1)S(1)}, bf16[2,16,2048]{2,1,0:T(8,128)(2,1)}, u32[]{:S(2)}) copy-start(bf16[2,16,2048]{2,1,0:T(8,128)(2,1)} %param.7) | copy-start | bytes 393220
  45.9 29.8 %all-to-all-start.4 = ((bf16[16,16,2048]{2,1,0:T(8,128)(2,1)}), bf16[16,16,2048]{2,1,0:T(8,128)(2,1)S(1)}, u32[]{:S(2)}, u32[]{:S(2)}) async-start(bf16[16,16,2048]{2,1,0:T(8,128)(2,1)} %bitcast.27), calls=%async_computation.4 | async-start | bytes 2097152 | tf_op jit(solution)/shard_map/all_to_all | solution.py:94
  51.5 29.9 %copy-start = (bf16[1,1024,2,384]{3,2,1,0:T(2,128)(2,1)S(1)}, bf16[1,1024,2,384]{3,2,1,0:T(2,128)(2,1)}, u32[]{:S(2)}) copy-start(bf16[1,1024,2,384]{3,2,1,0:T(2,128)(2,1)} %param.12) | copy-start | bytes 4718596
  51.5 32.5 %copy-start.10 = (s32[8]{0:T(128)S(1)}, s32[8]{0:T(128)}, u32[]{:S(2)}) copy-start(s32[8]{0:T(128)} %param.11) | copy-start | bytes 100
  75.8 5.6 %copy-start.6 = (bf16[16,16,2048]{2,1,0:T(8,128)(2,1)}, bf16[16,16,2048]{2,1,0:T(8,128)(2,1)S(1)}, u32[]{:S(2)}) copy-start(bf16[16,16,2048]{2,1,0:T(8,128)(2,1)S(1)} %all-to-all-done.4) | copy-start | bytes 3145732
  75.8 63.6 %all-to-all-start = ((bf16[16,16,2048]{2,1,0:T(8,128)(2,1)}), bf16[16,16,2048]{2,1,0:T(8,128)(2,1)}, u32[]{:S(2)}, u32[]{:S(2)}) async-start(bf16[16,16,2048]{2,1,0:T(8,128)(2,1)} %bitcast.4), calls=%async_computation | async-start | bytes 2097152 | tf_op jit(solution)/shard_map/all_to_all | solution.py:81
  81.4 110.9 %all-gather.7.cloned.1.call-start = ((), (), s32[]{:S(2)}) async-start(), calls=%async_computation.9 | async-start | bytes 2359296 | tf_op jit(solution)/shard_map/all_gather | solution.py:132
  81.4 102.4 %collective-permute-start = (bf16[1,1024,2,384]{3,2,0,1:T(2,128)(2,1)S(1)}, bf16[1,1024,2,384]{3,2,0,1:T(2,128)(2,1)S(1)}, u32[]{:S(2)}, u32[]{:S(2)}) collective-permute-start(bf16[1,1024,2,384]{3,2,0,1:T(2,128)(2,1)S(1)} %bitcast.119), channel_id=1, source_target_pairs={{0,8},{1,9},{2,10},{3,11},{4,12},{5,13},{6,14},{7,15},{8,0},{9,1},... | collective-permute-start | bytes 4718600 | tf_op jit(solution)/shard_map/ppermute | solution.py:10
  139.4 57.6 %all-to-all-start.6 = ((bf16[16,16,2048]{2,1,0:T(8,128)(2,1)}), bf16[16,16,2048]{2,1,0:T(8,128)(2,1)}, u32[]{:S(2)}, u32[]{:S(2)}) async-start(bf16[16,16,2048]{2,1,0:T(8,128)(2,1)} %bitcast.35), calls=%async_computation.6 | async-start | bytes 2097152 | tf_op jit(solution)/shard_map/all_to_all | solution.py:94
  145.4 127.3 %all-gather.9.cloned.1.call-start = ((), (), s32[]{:S(2)}) async-start(), calls=%async_computation.10 | async-start | bytes 4718592 | tf_op jit(solution)/shard_map/all_gather | solution.py:148
  197.0 7.5 %copy-start.1 = (bf16[1,1024,384]{2,1,0:T(8,128)(2,1)S(1)}, bf16[1,1024,384]{2,1,0:T(8,128)(2,1)}, u32[]{:S(2)}) copy-start(bf16[1,1024,384]{2,1,0:T(8,128)(2,1)} %param.13) | copy-start | bytes 2359300
  197.0 68.6 %all-to-all-start.5 = ((bf16[16,16,2048]{2,1,0:T(8,128)(2,1)}), bf16[16,16,2048]{2,1,0:T(8,128)(2,1)S(1)}, u32[]{:S(2)}, u32[]{:S(2)}) async-start(bf16[16,16,2048]{2,1,0:T(8,128)(2,1)} %bitcast.132), calls=%async_computation.5 | async-start | bytes 2097152 | tf_op jit(solution)/shard_map/all_to_all | solution.py:101
  204.4 58.0 %copy-start.11 = (f32[256,768]{1,0:T(8,128)S(1)}, f32[256,768]{1,0:T(8,128)}, u32[]{:S(2)}) copy-start(f32[256,768]{1,0:T(8,128)} %fusion.56) | copy-start | bytes 2359300
  204.4 87.2 %all-gather.11.cloned.1.call-start = ((), (), s32[]{:S(2)}) async-start(), calls=%async_computation.11 | async-start | bytes 2359296 | tf_op jit(solution)/shard_map/all_gather | solution.py:149
  204.5 56.9 %collective-permute-start.1 = (bf16[1,1024,384]{2,1,0:T(8,128)(2,1)S(1)}, bf16[1,1024,384]{2,1,0:T(8,128)(2,1)S(1)}, u32[]{:S(2)}, u32[]{:S(2)}) collective-permute-start(bf16[1,1024,384]{2,1,0:T(8,128)(2,1)S(1)} %copy-done.1), channel_id=1, source_target_pairs={{0,8},{1,9},{2,10},{3,11},{4,12},{5,13},{6,14},{7,15},{8,0},{9,1},... | collective-permute-start | bytes 2359304 | tf_op jit(solution)/shard_map/ppermute | solution.py:10
  265.6 31.3 %all-to-all-start.1 = ((bf16[16,16,2048]{2,1,0:T(8,128)(2,1)}), bf16[16,16,2048]{2,1,0:T(8,128)(2,1)S(1)}, u32[]{:S(2)}, u32[]{:S(2)}) async-start(bf16[16,16,2048]{2,1,0:T(8,128)(2,1)} %bitcast.8), calls=%async_computation.1 | async-start | bytes 2097152 | tf_op jit(solution)/shard_map/all_to_all | solution.py:86
  272.6 4.5 %copy-start.5 = (bf16[16,16,2048]{2,1,0:T(8,128)(2,1)S(1)}, bf16[16,16,2048]{2,1,0:T(8,128)(2,1)}, u32[]{:S(2)}) copy-start(bf16[16,16,2048]{2,1,0:T(8,128)(2,1)} %copy-done.4) | copy-start | bytes 3145732
  278.1 16.2 %copy-start.12 = (f32[256,768]{1,0:T(8,128)}, f32[256,768]{1,0:T(8,128)S(1)}, u32[]{:S(2)}) copy-start(f32[256,768]{1,0:T(8,128)S(1)} %fusion.57) | copy-start | bytes 2359300
  296.8 29.8 %all-to-all-start.7 = ((bf16[16,16,2048]{2,1,0:T(8,128)(2,1)}), bf16[16,16,2048]{2,1,0:T(8,128)(2,1)S(1)}, u32[]{:S(2)}, u32[]{:S(2)}) async-start(bf16[16,16,2048]{2,1,0:T(8,128)(2,1)} %bitcast.134), calls=%async_computation.7 | async-start | bytes 2097152 | tf_op jit(solution)/shard_map/all_to_all | solution.py:101
  326.7 29.9 %all-to-all-start.3 = ((bf16[16,16,2048]{2,1,0:T(8,128)(2,1)}), bf16[16,16,2048]{2,1,0:T(8,128)(2,1)}, u32[]{:S(2)}, u32[]{:S(2)}) async-start(bf16[16,16,2048]{2,1,0:T(8,128)(2,1)} %bitcast.133), calls=%async_computation.3 | async-start | bytes 2097152 | tf_op jit(solution)/shard_map/all_to_all | solution.py:86
  (3 other events, 5.3 us)
Sparse Core Ops, SparseCore 0:
  23.1 45.7 all-gather.4
  84.0 27.8 all-gather.6
  186.7 46.7 all-gather.8
  262.5 29.1 all-gather.10
where the time goes:
time: 368 us; the launch traced here: 366 us
  waiting for transfers between devices  248 us (67%)
  starting transfers between devices  54.3 us (15%)
  matrix products  30 us (8%)
  between operations  14.7 us (4%)
  local copies, waits for them, and re-layouts  10.2 us (3%)
  other arithmetic  8.4 us (2%)
    ppermute x2, waiting for transfers between devices, from_partner(): return lax.ppermute(value, axis, pairs)  92.8 us
    all_to_all x2, waiting for transfers between devices, run_micro(): lax.all_to_all(send_tokens, 'expert', split_axis=0, concat_axis=0, tiled=...  74.2 us
    all_to_all x2, waiting for transfers between devices, run_micro(): lax.all_to_all(expert_out.reshape(experts, item_count, model_width), 'exp...  23.2 us
    all_to_all x2, waiting for transfers between devices, run_micro(): lax.all_to_all(send_grads, 'expert', split_axis=0, concat_axis=0, tiled=T...  22.6 us
    all_to_all x2, waiting for transfers between devices, run_micro(): lax.all_to_all(row_input.reshape(experts, slots, model_width), 'expert',...  20.8 us
    all_gather x1, waiting for transfers between devices, local(): lax.all_gather(resident_down, 'dp', axis=1, tiled=True)  13.6 us
    all_to_all x2, starting transfers between devices, run_micro(): lax.all_to_all(row_input.reshape(experts, slots, model_width), 'expert',...  13 us
    all_to_all x2, starting transfers between devices, run_micro(): lax.all_to_all(expert_out.reshape(experts, item_count, model_width), 'exp...  12.6 us
  transfers between devices with their start and end apart: 14, of which 9 were waited for; matrix products, arithmetic and copies ran while one was open for 10% of the time, Pallas kernels for 0%

commit v1 on v0

--- a/solution.py
+++ b/solution.py
@@ -1,6 +1,10 @@
+import functools
+
 import jax
 import jax.numpy as jnp
 from jax import lax
+from jax.experimental import pallas as pl
+from jax.experimental.pallas import tpu as pltpu
 from jax.sharding import PartitionSpec as P
 
 
@@ -119,7 +123,337 @@
     return (hidden_out, input_grad)
 
 
-def local(hidden_in, cotangent, expert_ids, route_prob, swap_flags, gate_up, down_t):
+MESH = pl.DeviceIdType.MESH
+LANES = 128
+
+
+def dense_kernel(
+    experts,
+    replicas,
+    hidden_ref,
+    cot_ref,
+    ids_ref,
+    prob_ref,
+    gate_hbm,
+    down_hbm,
+    out_ref,
+    grad_ref,
+    other_gate,
+    other_down,
+    rows,
+    route,
+    gate_full,
+    down_full,
+    send_buf,
+    recv_buf,
+    total,
+    local_sem,
+    row_send,
+    row_recv,
+    route_send,
+    route_recv,
+    sum_send,
+    sum_recv,
+    weight_send,
+    weight_recv,
+    swap_send,
+    swap_recv,
+):
+    micro, tokens, width = hidden_ref.shape
+    hid = down_hbm.shape[1]
+    shard = gate_hbm.shape[0]
+    stages = experts.bit_length() - 1
+    half = experts // 2 * tokens
+    me = lax.axis_index("expert")
+    replica = lax.axis_index("dp")
+
+    def flip(bit):
+        return me + bit - 2 * bit * ((me // bit) % 2)
+
+    partners = [(replica, flip(experts >> (s + 1))) for s in range(stages)]
+    others = [(lax.rem(replica + r, replicas), me) for r in range(1, replicas)]
+
+    own_gate = pltpu.make_async_copy(gate_hbm, gate_full.at[replica], local_sem.at[0])
+    own_down = pltpu.make_async_copy(down_hbm, down_full.at[replica], local_sem.at[1])
+    own_gate.start()
+    own_down.start()
+
+    barrier = pltpu.get_barrier_semaphore()
+    for device in partners + others:
+        pl.semaphore_signal(barrier, inc=1, device_id=device, device_id_type=MESH)
+
+    lane = lax.broadcasted_iota(jnp.int32, (tokens, LANES), 1)
+    for m in range(micro):
+        rows[m, 0, 0:tokens, :] = hidden_ref[m]
+        rows[m, 1, 0:tokens, :] = cot_ref[m]
+        table = jnp.zeros((tokens, LANES), jnp.float32)
+        for k in range(ids_ref.shape[2]):
+            table = table + jnp.where(
+                lane == ids_ref[m, :, k : k + 1], prob_ref[m, :, k : k + 1], 0.0
+            )
+        route[m, 0:tokens, :] = table
+
+    pl.semaphore_wait(barrier, len(partners) + len(others))
+
+    def remote(src, dst, send, recv, device):
+        return pltpu.make_async_remote_copy(
+            src_ref=src,
+            dst_ref=dst,
+            send_sem=send,
+            recv_sem=recv,
+            device_id=device,
+            device_id_type=MESH,
+        )
+
+    def gather_stage(m, s):
+        held = (1 << s) * tokens
+        here, there = pl.ds(0, held), pl.ds(held, held)
+        return (
+            remote(
+                route.at[m, here],
+                route.at[m, there],
+                route_send.at[m, s],
+                route_recv.at[m, s],
+                partners[s],
+            ),
+            remote(
+                rows.at[m, :, here],
+                rows.at[m, :, there],
+                row_send.at[m, s],
+                row_recv.at[m, s],
+                partners[s],
+            ),
+        )
+
+    def sum_stage(m, s):
+        held = (1 << s) * tokens
+        part = pl.ds(held, held)
+        return remote(
+            send_buf.at[m, :, part],
+            recv_buf.at[m, :, part],
+            sum_send.at[m, s],
+            sum_recv.at[m, s],
+            partners[s],
+        )
+
+    gathers = [[gather_stage(m, s) for s in range(stages)] for m in range(micro)]
+    sums = [[sum_stage(m, s) for s in range(stages)] for m in range(micro)]
+    weights = []
+    for r, device in enumerate(others):
+        weights.append(
+            remote(
+                gate_hbm,
+                gate_full.at[replica],
+                weight_send.at[r, 0],
+                weight_recv.at[r, 0],
+                device,
+            )
+        )
+        weights.append(
+            remote(
+                down_hbm,
+                down_full.at[replica],
+                weight_send.at[r, 1],
+                weight_recv.at[r, 1],
+                device,
+            )
+        )
+    swaps = [
+        remote(gate_hbm, other_gate, swap_send.at[0], swap_recv.at[0], partners[0]),
+        remote(down_hbm, other_down, swap_send.at[1], swap_recv.at[1], partners[0]),
+    ]
+
+    def start(copies):
+        for copy in copies:
+            copy.start()
+
+    for m in range(micro):
+        start(gathers[m][0])
+    start(weights)
+    for s in range(stages):
+        for m in range(micro):
+            for copy in gathers[m][s]:
+                copy.wait_recv()
+            if s + 1 < stages:
+                start(gathers[m][s + 1])
+        if s == 0:
+            start(swaps)
+    own_gate.wait()
+    own_down.wait()
+    for copy in weights:
+        copy.wait_recv()
+
+    lane_full = lax.broadcasted_iota(jnp.int32, (half, LANES), 1)
+    contract_last = (((1,), (1,)), ((), ()))
+
+    def compute(m, upper):
+        first = half if upper else 0
+        block = pl.ds(first, half)
+        weight = jnp.sum(
+            jnp.where(lane_full == me, route[m, block, :], 0.0), axis=1, keepdims=True
+        )
+        projected = jnp.zeros((half, 2 * hid), jnp.float32)
+        d_hidden = jnp.zeros((half, hid), jnp.float32)
+        for r in range(replicas):
+            columns = pl.ds(r * shard, shard)
+            projected = projected + jnp.dot(
+                rows[m, 0, block, columns], gate_full[r], preferred_element_type=jnp.float32
+            )
+            row_grad = (weight * rows[m, 1, block, columns].astype(jnp.float32)).astype(
+                jnp.bfloat16
+            )
+            d_hidden = d_hidden + jnp.dot(
+                row_grad, down_full[r], preferred_element_type=jnp.float32
+            )
+        gate_part = projected[:, :hid]
+        upper_part = projected[:, hid:]
+        sigmoid_gate = jax.nn.sigmoid(gate_part)
+        hidden = (gate_part * sigmoid_gate * upper_part).astype(jnp.bfloat16)
+        d_gate = (
+            d_hidden * upper_part * sigmoid_gate * (1.0 + gate_part * (1.0 - sigmoid_gate))
+        ).astype(jnp.bfloat16)
+        d_upper = (d_hidden * gate_part * sigmoid_gate).astype(jnp.bfloat16)
+        d_joined = jnp.concatenate([d_gate, d_upper], axis=1)
+        step = min(512, shard)
+        for r in range(replicas):
+            for c in range(0, shard, step):
+                columns = pl.ds(r * shard + c, step)
+                output = lax.dot_general(
+                    hidden,
+                    down_full[r, c : c + step, :],
+                    contract_last,
+                    preferred_element_type=jnp.float32,
+                )
+                output = weight * output.astype(jnp.bfloat16).astype(jnp.float32)
+                row_input = lax.dot_general(
+                    d_joined,
+                    gate_full[r, c : c + step, :],
+                    contract_last,
+                    preferred_element_type=jnp.float32,
+                )
+                if upper:
+                    send_buf[m, 0, block, columns] = output.astype(jnp.bfloat16)
+                    send_buf[m, 1, block, columns] = row_input.astype(jnp.bfloat16)
+                else:
+                    total[m, 0, block, columns] = output
+                    total[m, 1, block, columns] = row_input.astype(jnp.bfloat16).astype(
+                        jnp.float32
+                    )
+
+    def reduce(m, s):
+        held = (1 << s) * tokens
+        sums[m][s].wait_recv()
+        if s == 0:
+            for i, ref in ((0, out_ref), (1, grad_ref)):
+                summed = total[m, i, 0:tokens, :] + recv_buf[m, i, tokens : 2 * tokens, :].astype(
+                    jnp.float32
+                )
+                ref[m] = summed.astype(jnp.bfloat16)
+            return
+        keep = held // 2
+        for i in range(2):
+            send_buf[m, i, keep:held, :] = (
+                total[m, i, keep:held, :]
+                + recv_buf[m, i, held + keep : 2 * held, :].astype(jnp.float32)
+            ).astype(jnp.bfloat16)
+        sums[m][s - 1].start()
+        for i in range(2):
+            total[m, i, 0:keep, :] = total[m, i, 0:keep, :] + recv_buf[
+                m, i, held : held + keep, :
+            ].astype(jnp.float32)
+
+    last = stages - 1
+    for m in range(micro):
+        compute(m, True)
+        sums[m][last].start()
+        compute(m, False)
+    for s in range(last, -1, -1):
+        for m in range(micro):
+            reduce(m, s)
+
+    for m in range(micro):
+        for s in range(stages):
+            for copy in gathers[m][s]:
+                copy.wait_send()
+            sums[m][s].wait_send()
+    for copy in weights:
+        copy.wait_send()
+    for copy in swaps:
+        copy.wait()
+
+
+def local_dense(hidden_in, cotangent, expert_ids, route_prob, swap_flags, gate_up, down_t):
+    experts = lax.axis_size("expert")
+    replicas = lax.axis_size("dp")
+    half_axis = experts // 2
+    my_index = lax.axis_index("expert")
+    flag_mine = jnp.sum(
+        jnp.where(jnp.arange(half_axis, dtype=jnp.int32) == my_index % half_axis, swap_flags, 0)
+    )
+    micro, tokens, width = hidden_in.shape
+    shard, hid = down_t.shape[1:]
+    stages = experts.bit_length() - 1
+    gate = gate_up.reshape(shard, 2 * hid)
+    down = down_t.reshape(shard, hid)
+    all_rows = experts * tokens
+    half_rows = all_rows // 2
+    vmem, anywhere = pl.BlockSpec(memory_space=pltpu.VMEM), pl.BlockSpec(memory_space=pl.ANY)
+    dma = pltpu.SemaphoreType.DMA
+    out, grad, other_gate, other_down = pl.pallas_call(
+        functools.partial(dense_kernel, experts, replicas),
+        out_shape=(
+            jax.ShapeDtypeStruct(hidden_in.shape, jnp.bfloat16),
+            jax.ShapeDtypeStruct(hidden_in.shape, jnp.bfloat16),
+            jax.ShapeDtypeStruct(gate.shape, jnp.bfloat16),
+            jax.ShapeDtypeStruct(down.shape, jnp.bfloat16),
+        ),
+        in_specs=[vmem] * 4 + [anywhere] * 2,
+        out_specs=[vmem, vmem, anywhere, anywhere],
+        scratch_shapes=[
+            pltpu.VMEM((micro, 2, all_rows, width), jnp.bfloat16),
+            pltpu.VMEM((micro, all_rows, LANES), jnp.float32),
+            pltpu.VMEM((replicas, shard, 2 * hid), jnp.bfloat16),
+            pltpu.VMEM((replicas, shard, hid), jnp.bfloat16),
+            pltpu.VMEM((micro, 2, all_rows, width), jnp.bfloat16),
+            pltpu.VMEM((micro, 2, all_rows, width), jnp.bfloat16),
+            pltpu.VMEM((micro, 2, half_rows, width), jnp.float32),
+            dma((2,)),
+            dma((micro, stages)),
+            dma((micro, stages)),
+            dma((micro, stages)),
+            dma((micro, stages)),
+            dma((micro, stages)),
+            dma((micro, stages)),
+            dma((replicas, 2)),
+            dma((replicas, 2)),
+            dma((2,)),
+            dma((2,)),
+        ],
+        compiler_params=pltpu.CompilerParams(
+            collective_id=0, has_side_effects=True, vmem_limit_bytes=50 * 2**20
+        ),
+        cost_estimate=pl.CostEstimate(
+            flops=micro * all_rows * width * hid * 12,
+            bytes_accessed=8 * shard * replicas * hid * 6,
+            transcendentals=micro * all_rows * hid,
+        ),
+    )(hidden_in, cotangent, expert_ids, route_prob, gate, down)
+    moved = flag_mine == 1
+    return (
+        out,
+        grad,
+        jnp.where(moved, other_gate.reshape(gate_up.shape), gate_up),
+        jnp.where(moved, other_down.reshape(down_t.shape), down_t),
+    )
+
+
+def pick_plan(mesh):
+    experts = mesh.shape["expert"]
+    small = experts <= 16 and experts & (experts - 1) == 0
+    return local_dense if small else local_routed
+
+
+def local_routed(hidden_in, cotangent, expert_ids, route_prob, swap_flags, gate_up, down_t):
     experts = lax.axis_size("expert")
     swap_bit = experts.bit_length() - 2
     half_axis = experts // 2
@@ -177,7 +511,7 @@
         P("expert", "dp", None),
     )
     return jax.shard_map(
-        local,
+        pick_plan(mesh),
         mesh=mesh,
         in_specs=placed,
         out_specs=(

time: 368 us -> 153 us (0.42)
  waiting for transfers between devices: 248 us -> 0 us
  Pallas kernels: 0 us -> 139 us
  starting transfers between devices: 54.3 us -> 0 us
  matrix products: 30 us -> 0 us
  between operations: 14.7 us -> 1.32 us
  other arithmetic: 8.4 us -> 4.35 us
    all_to_all x8 -> x0, waiting for transfers between devices: 141 us -> none  [the longest x2 74.2 us: run_micro(): lax.all_to_all(send_tokens, 'expert', split_axis=0, concat_axis=0, tiled=...]
    pallas_call x0 -> x1, Pallas kernels: none -> 139 us  [local_dense(): pl.pallas_call(functools.partial(dense_kernel, experts, replicas), out_sh...]
    ppermute x2 -> x0, waiting for transfers between devices: 92.8 us -> none  [from_partner(): return lax.ppermute(value, axis, pairs)]
    all_to_all x8 -> x0, starting transfers between devices: 49.2 us -> none  [the longest x2 13 us: run_micro(): lax.all_to_all(row_input.reshape(experts, slots, model_width), 'expert',...]
    dot_general x16 -> x0, matrix products: 30 us -> none  [the longest x2 6.57 us: expert_forward(): lax.dot_general(hidden, down_matrix, (((1,), (1,)), ((), ())), preferred_...]
    all_gather x4 -> x0, waiting for transfers between devices: 13.6 us -> none  [the longest x1 13.6 us: local(): lax.all_gather(resident_down, 'dp', axis=1, tiled=True)]
    ppermute x2 -> x0, starting transfers between devices: 4.91 us -> none  [from_partner(): return lax.ppermute(value, axis, pairs)]
    unnamed x28 -> x13, local copies, waits for them, and re-layouts: 8.07 us -> 5.82 us
  transfers between devices with their start and end apart: 14 -> 0, of which waited for: 9 -> 0; matrix products, arithmetic and copies ran while one was open for 10% -> 0% of each run, Pallas kernels for 0% -> 0%
where the time goes in v1:
time: 153 us; the launch traced here: 152 us
  Pallas kernels  139 us (91%)
  local copies, waits for them, and re-layouts  7.15 us (5%)
  other arithmetic  4.35 us (3%)
    pallas_call x1, Pallas kernels, local_dense(): pl.pallas_call(functools.partial(dense_kernel, experts, replicas), out_sh...  139 us
    unnamed x13, local copies, waits for them, and re-layouts  5.82 us

profile of v1, /device:TPU:8, one launch (start us, length us, event | category | flops | bytes accessed | tf_op | source)
XLA Modules:
  0.0 152.2 jit_solution(16380634280617919648)
XLA Ops:
  0.6 0.8 copy.11.ids_ref
  1.4 0.8 copy.12.prob_ref
  2.2 0.0 copy-start
  2.2 0.0 copy-start.1
  2.2 0.0 copy-start.2
  2.2 3.0 %copy.13 = bf16[128,8,2,384]{3,1,2,0:T(8,128)(2,1)} copy(bf16[128,8,2,384]{3,2,1,0:T(2,128)(2,1)} %bitcast.10) | data formatting | bytes 3145728
  5.1 0.0 copy-done
  5.1 0.0 copy-done.1
  5.1 0.0 copy-done.2
  5.1 139.4 %shard_map.102 = (bf16[2,16,2048]{2,1,0:T(8,128)(2,1)S(1)}, bf16[2,16,2048]{2,1,0:T(8,128)(2,1)S(1)}, bf16[1024,768]{1,0:T(8,128)(2,1)S(1)}, bf16[1024,384]{1,0:T(8,128)(2,1)S(1)}) custom-call(bf16[2,16,2048]{2,1,0:T(8,128)(2,1)S(1)} %copy-done.1, bf16[2,16,2048]{2,1,0:T(8,128)(2,1)S(1)} %copy-done.2, s32[2,16,8]{2,1,0:T(8,128)S(1)} %copy.11.ids_ref, ...), custom_call_target="tpu_custom_call" | custom-call | flops 4831838208 | bytes 37748736 | tf_op jit(solution)/shard_map/pallas_call | solution.py:402
  144.6 0.0 copy-start.3
  144.6 1.3 reshape.22
  145.9 0.0 copy-done.3
  145.9 0.6 fusion
  147.2 2.7 %broadcast_select_fusion = bf16[1,256,8,384]{3,2,1,0:T(8,128)(2,1)} fusion(bf16[1,256,8,384]{3,2,1,0:T(8,128)(2,1)} %bitcast.12, bf16[1,256,8,384]{3,2,1,0:T(8,128)(2,1)} %bitcast.11, pred[]{:T(512)S(6)} %eq.13), kind=kLoop, calls=%fused_computation | loop fusion | flops 786432 | bytes 4718593 | tf_op jit(solution)/shard_map/jit(_where)/select_n | solution.py:445
  150.0 1.0 bitcast_select_fusion
  150.9 0.7 copy.16
  151.6 0.7 copy.17
Async XLA Ops:
  2.2 3.0 %copy-start = (bf16[1,1024,384]{2,1,0:T(8,128)(2,1)S(1)}, bf16[1,1024,384]{2,1,0:T(8,128)(2,1)}, u32[]{:S(2)}) copy-start(bf16[1,1024,384]{2,1,0:T(8,128)(2,1)} %param.13) | copy-start | bytes 2359300
  2.2 3.0 %copy-start.1 = (bf16[2,16,2048]{2,1,0:T(8,128)(2,1)S(1)}, bf16[2,16,2048]{2,1,0:T(8,128)(2,1)}, u32[]{:S(2)}) copy-start(bf16[2,16,2048]{2,1,0:T(8,128)(2,1)} %hidden_ref.1) | copy-start | bytes 393220
  2.2 3.0 %copy-start.2 = (bf16[2,16,2048]{2,1,0:T(8,128)(2,1)S(1)}, bf16[2,16,2048]{2,1,0:T(8,128)(2,1)}, u32[]{:S(2)}) copy-start(bf16[2,16,2048]{2,1,0:T(8,128)(2,1)} %cot_ref.1) | copy-start | bytes 393220
  144.6 1.4 copy-start.3
